TPU v7x, 512 devices: a whole 4x8x8 slice. The times are simulated.
512 devices in a mesh: row: 32 (over x_lo, z, core), aisle: 16 (over y, x_hi).
Axes of the slice: x: 4 (x_hi: 2, x_lo: 2; x = x_hi * 2 + x_lo), y: 8, z: 8, core: 2. Of those that a mesh axis runs over, the one named last changes fastest.
Arguments:
- flow_state: bfloat16 [64, 256, 32, 256], P('row', 'aisle'), may hold values from -6 to 6
- mode_weight: bfloat16 [2, 64, 64, 32, 1024], P(None, 'row', 'aisle'), may hold values from -4 to 4
- bypass_weight: bfloat16 [32, 32], replicated, may hold values from -1 to 1
- bias_term: float32 [32], replicated, may hold values from -1 to 1
Outputs:
- mixed_field: bfloat16 [64, 256, 32, 256], P('row', 'aisle')
All inputs are finite; a program needn't handle non-finite values.
Results may differ from a plain program's by a relative error of at most 0.025.
Values may be sent and summed in bfloat16 or wider, within the bound.
A program may use at most 64 MiB of HBM per device.

v0:
```python
import math

import jax
import jax.numpy as jnp
from jax import lax
from jax.sharding import PartitionSpec as P

MX = 64
MY = 64
MZ = 32


def twiddle(frequencies, positions, length):
    phase_index = jnp.mod(frequencies[:, None] * positions[None, :], length).astype(jnp.float32)
    angles = phase_index * (2.0 * math.pi / length)
    return (jnp.cos(angles).astype(jnp.bfloat16), jnp.sin(angles).astype(jnp.bfloat16))


def height_tables(height):
    frequencies = jnp.arange(MZ, dtype=jnp.int32)
    positions = jnp.arange(height, dtype=jnp.int32)
    phase_index = jnp.mod(frequencies[:, None] * positions[None, :], height).astype(jnp.float32)
    angles = phase_index * (2.0 * math.pi / height)
    cos_height = jnp.cos(angles)
    sin_height = jnp.sin(angles)
    forward = jnp.concatenate([cos_height, -sin_height], 0).T.astype(jnp.bfloat16)
    weights = jnp.where(frequencies == 0, 1.0, 2.0).astype(jnp.float32)[:, None]
    inverse = jnp.concatenate([weights * cos_height, -weights * sin_height], 0).astype(jnp.bfloat16)
    return (forward, inverse)


def contract(pattern, left, right):
    return jnp.einsum(pattern, left, right, preferred_element_type=jnp.float32)


def y_forward(cos_table, sin_table, real_part, imag_part):
    pattern = "qy,xyck->qxck"
    out_real = contract(pattern, cos_table, real_part) + contract(pattern, sin_table, imag_part)
    out_imag = contract(pattern, cos_table, imag_part) - contract(pattern, sin_table, real_part)
    return jnp.stack([out_real, out_imag], 1)


def y_inverse(cos_table, sin_table, real_part, imag_part):
    pattern = "yq,xqok->xyok"
    out_real = contract(pattern, cos_table, real_part) - contract(pattern, sin_table, imag_part)
    out_imag = contract(pattern, cos_table, imag_part) + contract(pattern, sin_table, real_part)
    return jnp.stack([out_real, out_imag], 3)


def on_device(flow_state, mode_weight, bypass_weight, bias_term):
    width_x, width_y, channels, height = flow_state.shape
    rows_x = lax.axis_size("row")
    rows_y = lax.axis_size("aisle")
    total_x = width_x * rows_x
    total_y = width_y * rows_y
    local_y = lax.axis_index("aisle") * width_y + jnp.arange(width_y, dtype=jnp.int32)
    all_x = jnp.arange(total_x, dtype=jnp.int32)
    scaling = 1.0 / math.sqrt(total_x * total_y * height)
    forward_z, inverse_z = height_tables(height)
    z_spectrum = jnp.dot(
        flow_state.reshape(-1, height), forward_z, preferred_element_type=jnp.float32
    )
    z_spectrum = z_spectrum.astype(jnp.bfloat16).reshape(width_x, width_y, channels, 2, MZ)
    z_real = z_spectrum[:, :, :, 0]
    z_imag = z_spectrum[:, :, :, 1]
    cos_table, sin_table = twiddle(
        jnp.arange(MY // rows_y * lax.axis_size("aisle"), dtype=jnp.int32) - MY // 2,
        local_y,
        total_y,
    )
    y_sums = lax.psum_scatter(
        y_forward(cos_table, sin_table, z_real, z_imag).astype(jnp.bfloat16),
        "aisle",
        scatter_dimension=0,
        tiled=True,
    )
    modes_x = mode_weight.shape[1]
    modes_y = mode_weight.shape[2]
    cos_xfull, sin_xfull = twiddle(jnp.arange(MX, dtype=jnp.int32) - MX // 2, all_x, total_x)
    flat_sums = y_sums.reshape(modes_y, 2, width_x, channels * MZ)
    incoming = lax.all_to_all(flat_sums, "row", split_axis=3, concat_axis=2, tiled=True)
    pattern = "px,qxs->pqs"
    out_real = contract(pattern, cos_xfull, incoming[:, 0]) + contract(
        pattern, sin_xfull, incoming[:, 1]
    )
    out_imag = contract(pattern, cos_xfull, incoming[:, 1]) - contract(
        pattern, sin_xfull, incoming[:, 0]
    )
    full_sum = (jnp.stack([out_real, out_imag], 1) * scaling).astype(jnp.bfloat16)
    mode_flat = lax.all_to_all(full_sum, "row", split_axis=0, concat_axis=3, tiled=True)
    mode_sums = mode_flat.reshape(modes_x, 2, modes_y, channels, MZ)
    weights = mode_weight.reshape(2, modes_x, modes_y, MZ, channels, channels)
    pattern_mix = "pqck,pqkco->pqok"
    mixed_real = contract(pattern_mix, mode_sums[:, 0], weights[0]) - contract(
        pattern_mix, mode_sums[:, 1], weights[1]
    )
    mixed_imag = contract(pattern_mix, mode_sums[:, 0], weights[1]) + contract(
        pattern_mix, mode_sums[:, 1], weights[0]
    )
    mode_mixed = jnp.stack([mixed_real, mixed_imag], 1).astype(jnp.bfloat16)
    cos_xback, sin_xback = twiddle(all_x, jnp.arange(MX, dtype=jnp.int32) - MX // 2, total_x)
    flat_mixed = mode_mixed.reshape(modes_x, 2, modes_y, channels * MZ)
    incoming = lax.all_to_all(flat_mixed, "row", split_axis=3, concat_axis=0, tiled=True)
    pattern = "xp,pqs->xqs"
    out_real = contract(pattern, cos_xback, incoming[:, 0]) - contract(
        pattern, sin_xback, incoming[:, 1]
    )
    out_imag = contract(pattern, cos_xback, incoming[:, 1]) + contract(
        pattern, sin_xback, incoming[:, 0]
    )
    full_sum = jnp.stack([out_real, out_imag], 0).astype(jnp.bfloat16)
    back_flat = lax.all_to_all(full_sum, "row", split_axis=1, concat_axis=3, tiled=True)
    back_x = back_flat.reshape(2, width_x, modes_y, channels, MZ)
    incoming = lax.all_gather(back_x, "aisle", axis=2, tiled=True)
    number = incoming.shape[2]
    cos_table, sin_table = twiddle(local_y, jnp.arange(number, dtype=jnp.int32) - MY // 2, total_y)
    back_y = y_inverse(cos_table, sin_table, incoming[0], incoming[1]).astype(jnp.bfloat16)
    spectral = jnp.dot(back_y.reshape(-1, 2 * MZ), inverse_z, preferred_element_type=jnp.float32)
    spectral = spectral.reshape(width_x, width_y, channels, height) * scaling
    bypass = jnp.einsum(
        "xyiz,io->xyoz", flow_state, bypass_weight, preferred_element_type=jnp.float32
    )
    return jax.nn.gelu(spectral + bypass + bias_term[None, None, :, None]).astype(jnp.bfloat16)


def solution(mesh):
    in_specs = (P("row", "aisle", None, None), P(None, "row", "aisle", None, None), P(), P())
    out_specs = P("row", "aisle", None, None)
    return jax.shard_map(
        on_device, mesh=mesh, in_specs=in_specs, out_specs=out_specs, check_vma=False
    )
```

profile of v0, /device:TPU:1, one launch (start us, length us, event | category | flops | bytes accessed | tf_op | source)
XLA Modules:
  0.0 395.3 jit_solution(8878935872751583948)
XLA Ops:
  11.1 3.9 copy.62
  15.0 213.5 %reduce-scatter.2.cloned.1.call-done = bf16[4,2,2,32,32]{4,3,2,1,0:T(8,128)(2,1)} async-done(((bf16[64,2,2,32,32]{4,3,2,1,0:T(8,128)(2,1)}), bf16[4,2,2,32,32]{4,3,2,1,0:T(8,128)(2,1)}) %reduce-scatter.2.cloned.1.call-update) | async-done | bytes 32784 | tf_op jit(solution)/shard_map/reduce_scatter | solution.py:71
  228.5 2.4 copy.112
  230.9 2.6 reshape.90
  233.5 13.4 %all-to-all-start = ((bf16[32,2,256]{2,1,0:T(2,128)(2,1)}), bf16[32,2,256]{2,1,0:T(2,128)(2,1)S(1)}, u32[]{:S(2)}, u32[]{:S(2)}) async-start(bf16[32,2,256]{2,1,0:T(2,128)(2,1)} %reshape.90), calls=%async_computation.1 | async-start | bytes 65536 | tf_op jit(solution)/shard_map/all_to_all | solution.py:81
  247.8 2.8 squeeze.49
  250.7 2.6 squeeze.51
  253.3 1.5 all-to-all-done
  254.8 3.2 reshape.91
  258.0 2.9 copy.113
  263.5 6.8 %all-to-all-start.1 = ((bf16[32,2,256]{2,1,0:T(2,128)(2,1)}), bf16[32,2,256]{2,1,0:T(2,128)(2,1)S(1)}, u32[]{:S(2)}, u32[]{:S(2)}) async-start(bf16[32,2,256]{2,1,0:T(2,128)(2,1)} %reshape.92), calls=%async_computation.2 | async-start | bytes 65536 | tf_op jit(solution)/shard_map/all_to_all | solution.py:90
  270.3 7.9 %all-to-all-done.1 = bf16[32,2,256]{2,1,0:T(2,128)(2,1)S(1)} async-done(((bf16[32,2,256]{2,1,0:T(2,128)(2,1)}), bf16[32,2,256]{2,1,0:T(2,128)(2,1)S(1)}, u32[]{:S(2)}, u32[]{:S(2)}) %all-to-all-start.1) | async-done | bytes 32800 | tf_op jit(solution)/shard_map/all_to_all | solution.py:90
  278.7 5.8 %fusion = (f32[2,4,32,32]{3,2,1,0:T(8,128)S(1)}, f32[2,4,32,32]{3,2,1,0:T(8,128)S(1)}, f32[2,4,32,32]{3,2,1,0:T(8,128)S(1)}, f32[2,4,32,32]{3,2,1,0:T(8,128)S(1)}) fusion(bf16[2,4,32,32,32]{4,3,2,1,0:T(8,128)(2,1)S(1)} %squeeze.49, f32[2,4,32,32]{3,2,1,0:T(8,128)S(1)} %copy.124, f32[2,4,32,32]{3,2,1,0:T(8,128)S(1)} %copy.125, ...), kind=kLoop, calls=%fused_computation.4 | loop fusion | flops 2588672 | bytes 1245184
  286.2 2.6 reshape.94
  288.8 4.4 %all-to-all-start.2 = ((bf16[32,2,256]{2,1,0:T(2,128)(2,1)}), bf16[32,2,256]{2,1,0:T(2,128)(2,1)S(1)}, u32[]{:S(2)}, u32[]{:S(2)}) async-start(bf16[32,2,256]{2,1,0:T(2,128)(2,1)} %reshape.94), calls=%async_computation.3 | async-start | bytes 65536 | tf_op jit(solution)/shard_map/all_to_all | solution.py:103
  293.2 8.0 %all-to-all-done.2 = bf16[32,2,256]{2,1,0:T(2,128)(2,1)S(1)} async-done(((bf16[32,2,256]{2,1,0:T(2,128)(2,1)}), bf16[32,2,256]{2,1,0:T(2,128)(2,1)S(1)}, u32[]{:S(2)}, u32[]{:S(2)}) %all-to-all-start.2) | async-done | bytes 32800 | tf_op jit(solution)/shard_map/all_to_all | solution.py:103
  301.2 2.2 reshape.95
  303.5 2.0 copy.114
  307.8 4.4 %all-to-all-start.3 = ((bf16[32,2,256]{2,1,0:T(2,128)(2,1)}), bf16[32,2,256]{2,1,0:T(2,128)(2,1)S(1)}, u32[]{:S(2)}, u32[]{:S(2)}) async-start(bf16[32,2,256]{2,1,0:T(2,128)(2,1)} %reshape.96), calls=%async_computation.4 | async-start | bytes 65536 | tf_op jit(solution)/shard_map/all_to_all | solution.py:112
  312.4 7.9 %all-to-all-done.3 = bf16[32,2,256]{2,1,0:T(2,128)(2,1)S(1)} async-done(((bf16[32,2,256]{2,1,0:T(2,128)(2,1)}), bf16[32,2,256]{2,1,0:T(2,128)(2,1)S(1)}, u32[]{:S(2)}, u32[]{:S(2)}) %all-to-all-start.3) | async-done | bytes 32800 | tf_op jit(solution)/shard_map/all_to_all | solution.py:112
  320.5 59.1 %all_gather.3 = bf16[2,2,64,32,32]{4,3,1,0,2:T(8,128)(2,1)S(1)} all-gather(bf16[2,2,4,32,32]{4,3,1,0,2:T(8,128)(2,1)S(1)} %copy.77), channel_id=1, replica_groups=mesh['row'=32,'aisle'=16] {'aisle'}, dimensions={2}, use_global_device_ids=true | all-gather | bytes 557056 | tf_op jit(solution)/shard_map/all_gather | solution.py:114
  380.0 1.2 copy.122
  382.0 1.2 copy.123
  387.1 1.4 fusion.22
  (80 shorter events, 17.8 us)
Async XLA Ops:
  6.5 1.0 copy-start
  6.5 222.0 %reduce-scatter.2.cloned.1.call-start = ((), (), s32[]{:S(2)}) async-start(), calls=%async_computation.5 | async-start | bytes 2228224 | tf_op jit(solution)/shard_map/reduce_scatter | solution.py:71
  15.0 231.9 %copy-start.1 = (bf16[2,2,4,32,1024]{4,3,2,1,0:T(8,128)(2,1)S(1)}, bf16[2,2,4,32,1024]{4,3,2,1,0:T(8,128)(2,1)}, u32[]{:S(2)}) copy-start(bf16[2,2,4,32,1024]{4,3,2,1,0:T(8,128)(2,1)} %param.5) | copy-start | bytes 3145732
  233.5 21.3 %all-to-all-start = ((bf16[32,2,256]{2,1,0:T(2,128)(2,1)}), bf16[32,2,256]{2,1,0:T(2,128)(2,1)S(1)}, u32[]{:S(2)}, u32[]{:S(2)}) async-start(bf16[32,2,256]{2,1,0:T(2,128)(2,1)} %reshape.90), calls=%async_computation.1 | async-start | bytes 65536 | tf_op jit(solution)/shard_map/all_to_all | solution.py:81
  263.5 14.7 %all-to-all-start.1 = ((bf16[32,2,256]{2,1,0:T(2,128)(2,1)}), bf16[32,2,256]{2,1,0:T(2,128)(2,1)S(1)}, u32[]{:S(2)}, u32[]{:S(2)}) async-start(bf16[32,2,256]{2,1,0:T(2,128)(2,1)} %reshape.92), calls=%async_computation.2 | async-start | bytes 65536 | tf_op jit(solution)/shard_map/all_to_all | solution.py:90
  288.8 12.4 %all-to-all-start.2 = ((bf16[32,2,256]{2,1,0:T(2,128)(2,1)}), bf16[32,2,256]{2,1,0:T(2,128)(2,1)S(1)}, u32[]{:S(2)}, u32[]{:S(2)}) async-start(bf16[32,2,256]{2,1,0:T(2,128)(2,1)} %reshape.94), calls=%async_computation.3 | async-start | bytes 65536 | tf_op jit(solution)/shard_map/all_to_all | solution.py:103
  307.8 12.5 %all-to-all-start.3 = ((bf16[32,2,256]{2,1,0:T(2,128)(2,1)}), bf16[32,2,256]{2,1,0:T(2,128)(2,1)S(1)}, u32[]{:S(2)}, u32[]{:S(2)}) async-start(bf16[32,2,256]{2,1,0:T(2,128)(2,1)} %reshape.96), calls=%async_computation.4 | async-start | bytes 65536 | tf_op jit(solution)/shard_map/all_to_all | solution.py:112
  385.9 1.2 copy-start.2
  385.9 1.2 copy-start.3
Sparse Core Ops, SparseCore 0:
  15.2 213.2 reduce-scatter.1
where the time goes:
time: 402 us; the launch traced here: 395 us
  waiting for transfers between devices  239 us (59%)
  blocking collectives  59.1 us (15%)
  local copies, waits for them, and re-layouts  38.4 us (10%)
  starting transfers between devices  29 us (7%)
  between operations  13.9 us (3%)
  matrix products  9.43 us (2%)
  other arithmetic  6.72 us (2%)
    reduce_scatter x1, waiting for transfers between devices, on_device(): lax.psum_scatter(y_forward(cos_table, sin_table, z_real, z_imag).astype(j...  213 us
    all_gather x1, blocking collectives, on_device(): incoming = lax.all_gather(back_x, 'aisle', axis=2, tiled=True)  59.1 us
    unnamed x26, local copies, waits for them, and re-layouts  17.2 us
    all_to_all x1, starting transfers between devices, on_device(): lax.all_to_all(flat_sums, 'row', split_axis=3, concat_axis=2, tiled=True)  13.4 us
  transfers between devices with their start and end apart: 5, of which 5 were waited for; matrix products, arithmetic and copies ran while one was open for 2% of the time, Pallas kernels for 0%

commit v1 on v0

v1 whole, which is shorter than its diff:
```python
import math

import jax
import jax.numpy as jnp
import numpy as np
from jax import lax
from jax.experimental import pallas as pl
from jax.experimental.pallas import tpu as pltpu
from jax.sharding import PartitionSpec as P

C = 32
MX = 64
MY = 64
MZ = 32
NX = 64
NY = 256
NZ = 256
NR = 32
NA = 16
SCALING = 1.0 / math.sqrt(NX * NY * NZ)
BF = jnp.bfloat16
F32 = jnp.float32
MESH = pl.DeviceIdType.MESH


def twiddle(frequencies, positions, length):
    phase = np.mod(frequencies[:, None] * positions[None, :], length).astype(np.float32)
    angles = phase * np.float32(2.0 * math.pi / length)
    return np.cos(angles), np.sin(angles)


def tables():
    cz, sz = twiddle(np.arange(MZ), np.arange(NZ), NZ)
    weight = np.where(np.arange(MZ) == 0, 1.0, 2.0).astype(np.float32)[:, None]
    forward = np.stack([cz, -sz], 0)
    inverse = np.stack([weight * cz, -weight * sz], 0)
    fz = np.zeros((2, 2, NZ, 2, 2, 2, MZ), np.float32)
    iz = np.zeros((2, 2, 2, 2, 2, MZ, NZ), np.float32)
    for x in range(2):
        for c in range(2):
            fz[x, c, :, :, c, x, :] = forward.transpose(2, 0, 1)
            iz[x, c, :, c, x] = inverse
    fz = fz.reshape(4, 256, 256)
    iz = iz.reshape(4, 256, 256)
    eye = np.eye(16, dtype=np.float32)
    perm = np.einsum("ab,cd->acdb", eye, eye).reshape(256, 256)
    cy, sy = twiddle(np.arange(MY) - MY // 2, np.arange(NY), NY)
    ty = np.stack([np.stack([cy, sy]), np.stack([-sy, cy])])
    t1 = ty.reshape(2, 2, 32, 2, NY).transpose(3, 2, 0, 1, 4).reshape(128, 512)
    cx, sx = twiddle(np.arange(MX) - MX // 2, np.arange(NX), NX)
    tx = np.stack([np.stack([cx, sx]), np.stack([-sx, cx])])
    t2 = tx.reshape(2, 2, MX, 32, 2).transpose(2, 0, 4, 3, 1).reshape(128, 128)
    bx = np.stack([np.stack([cx, -sx]), np.stack([sx, cx])])
    t3 = bx.reshape(2, 2, MX, 32, 2).transpose(4, 3, 0, 2, 1).reshape(128, 128)
    by = np.stack([np.stack([cy, -sy]), np.stack([sy, cy])])
    t4 = by.reshape(2, 2, 32, 2, NY).transpose(0, 4, 3, 2, 1).reshape(512, 128)
    spread = np.einsum("ab,cd,o->acdbo", eye, np.eye(4), np.ones(32)).reshape(64, 2048)
    fold = np.einsum("lm,ab,cd,g->lacdgmb", np.eye(2), eye, np.eye(4), np.ones(4)).reshape(128, 512)
    return [jnp.asarray(t, BF) for t in (fz, perm, t1, t2, spread, fold, t3, t4, iz)]


def dot(left, right):
    return jnp.dot(left, right, preferred_element_type=F32)


def dot_tn(left, right):
    return lax.dot_general(left, right, (((0,), (0,)), ((), ())), preferred_element_type=F32)


def dot_nt(left, right):
    return lax.dot_general(left, right, (((1,), (1,)), ((), ())), preferred_element_type=F32)


def exchange_halves(first, second, roll):
    low = (lax.broadcasted_iota(jnp.int32, first.shape, 1) & 32) == 0
    return (
        jnp.where(low, first, roll(second, 32, 1)),
        jnp.where(low, roll(first, 96, 1), second),
    )


def stage_z(flow, fz, perm):
    total = None
    for x in range(2):
        for c in range(2):
            part = dot(flow[x, :, c * 16 : c * 16 + 16, :].reshape(256, 256), fz[2 * x + c])
            total = part if total is None else total + part
    return dot(perm, total.astype(BF)).astype(BF)


def stage_y(gathered, t1, roll):
    sums = dot(t1, jnp.concatenate([gathered[:, :128], gathered[:, 128:]], 0))
    return exchange_halves(sums[:64], sums[64:], roll)


def stage_mix(modes, spread, fold, weight):
    planes = []
    for p in range(2):
        wide = dot_tn(modes, spread[:, p * 1024 : p * 1024 + 1024])
        real = [None, None]
        imag = [None, None]
        for q in range(2):
            for c in range(2):
                rows = slice(c * 64 + q * 32, c * 64 + q * 32 + 32)
                for h in range(4):
                    mr = wide[rows, h * 128 : h * 128 + 128]
                    mi = wide[rows, 512 + h * 128 : 512 + h * 128 + 128]
                    wr = weight(0, p, q, c * 512 + h * 128).astype(F32)
                    wi = weight(1, p, q, c * 512 + h * 128).astype(F32)
                    re = mr * wr - mi * wi
                    im = mr * wi + mi * wr
                    real[q] = re if real[q] is None else real[q] + re
                    imag[q] = im if imag[q] is None else imag[q] + im
        planes += [jnp.concatenate(real, 0), jnp.concatenate(imag, 0)]
    total = jnp.concatenate(planes, 1)
    high = total.astype(BF)
    low = (total - high.astype(F32)).astype(BF)
    mixed = dot_nt(fold, high) + dot_nt(fold, low)
    return jnp.concatenate([mixed[:64], mixed[64:]], 1)


def stage_y_back(first, second, t4, roll):
    low, high = exchange_halves(first.astype(F32), second.astype(F32), roll)
    return dot(t4, jnp.concatenate([low, high], 0).astype(BF))


def bypass_matrix(bypass, lanes):
    wide = dot(bypass, lanes).astype(BF)
    tall = jnp.concatenate([wide] * 8, 0)
    rows = lax.broadcasted_iota(jnp.int32, (256, 256), 0) // 32
    columns = lax.broadcasted_iota(jnp.int32, (256, 256), 1) // 32
    return jnp.where(rows == columns, tall, jnp.zeros_like(tall))


def stage_z_back(planes, perm, iz, bypass, store):
    rows = dot(perm, planes).astype(BF)
    for x in range(2):
        for o in range(2):
            spectral = dot(rows, iz[2 * x + o]) * SCALING
            total = spectral.reshape(16, 16, 256) + bypass(x, o)
            store(x, o, jax.nn.gelu(total).astype(BF))


def kernel(
    flow, weight, bypass, bias, fz, perm, t1, t2, spread, fold, t3, t4, iz,
    out,
    send_a, recv_a, send_b, recv_b, send_c, recv_c, send_d, recv_d, send_e, recv_e, send_f, recv_f,
    plain, send_sem, recv_sem, own_sem,
):
    row = lax.axis_index("row")
    aisle = lax.axis_index("aisle")
    quad = row // 2
    half = row % 2
    barrier = pltpu.get_barrier_semaphore()

    @pl.loop(1, NA)
    def _(i):
        pl.semaphore_signal(barrier, inc=1, device_id=(row, lax.rem(aisle + i, NA)), device_id_type=MESH)

    @pl.loop(1, NR)
    def _(i):
        pl.semaphore_signal(barrier, inc=1, device_id=(lax.rem(row + i, NR), aisle), device_id_type=MESH)

    send_a[...] = stage_z(flow, fz, perm[...]).reshape(16, 16, 256)
    pl.semaphore_wait(barrier, NA - 1 + NR - 1)

    def remote(stage, source, target, device):
        pltpu.make_async_remote_copy(
            src_ref=source,
            dst_ref=target,
            send_sem=send_sem.at[stage],
            recv_sem=recv_sem.at[stage],
            device_id=device,
            device_id_type=MESH,
        ).start()

    def local(stage, source, target):
        pltpu.make_async_copy(source, target, recv_sem.at[stage]).start()

    def arrived(stage, whole):
        pltpu.make_async_copy(whole, whole, recv_sem.at[stage]).wait()

    def sent(stage, part):
        pltpu.make_async_copy(part, part, send_sem.at[stage]).wait()

    local(0, send_a.at[aisle], recv_a.at[aisle])

    @pl.loop(1, NA)
    def _(i):
        to = lax.rem(aisle + i, NA)
        remote(0, send_a.at[to], recv_a.at[aisle], (row, to))

    lanes = (
        lax.broadcasted_iota(jnp.int32, (32, 256), 0)
        == lax.broadcasted_iota(jnp.int32, (32, 256), 1) % 32
    ).astype(F32).astype(BF)
    diagonal = bypass_matrix(bypass[...], lanes)
    eye = lax.broadcasted_iota(jnp.int32, (32, 32), 0) == lax.broadcasted_iota(jnp.int32, (32, 32), 1)
    column = jnp.sum(jnp.where(eye, bias[...], 0.0), axis=1, keepdims=True)
    tall = jnp.concatenate([column] * 8, 0)
    for x in range(2):
        for y in range(2):
            field = flow[x, y * 8 : y * 8 + 8].reshape(256, 256)
            plain[x, y * 8 : y * 8 + 8] = (dot_tn(diagonal, field) + tall).reshape(8, 32, 256)

    arrived(0, recv_a)
    first, second = stage_y(recv_a[...].reshape(256, 256), t1[...], pltpu.roll)
    send_b.reshape(128, 128)[:64] = first.astype(BF)
    send_b.reshape(128, 128)[64:] = second.astype(BF)

    local(1, send_b.at[:, row], recv_b.at[:, row])

    @pl.loop(1, NR)
    def _(i):
        to = lax.rem(row + i, NR)
        remote(1, send_b.at[:, to], recv_b.at[:, row], (to, aisle))

    arrived(1, recv_b)
    modes = dot(t2[...], recv_b.reshape(128, 128)[...]) * SCALING
    send_c.reshape(128, 128)[...] = modes.astype(BF)

    mine = quad == aisle
    slot = half * 16 + aisle

    @pl.when(mine)
    def _():
        local(2, send_c.at[row], recv_c.at[slot])

    @pl.when(jnp.logical_not(mine))
    def _():
        pltpu.make_async_remote_copy(
            src_ref=send_c.at[row],
            dst_ref=recv_c.at[slot],
            send_sem=own_sem,
            recv_sem=recv_sem.at[2],
            device_id=(row, quad),
            device_id_type=MESH,
        ).start()

    @pl.loop(1, NR)
    def _(i):
        to = lax.rem(row + i, NR)
        remote(2, send_c.at[to], recv_c.at[slot], (to, quad))

    arrived(2, recv_c)

    @pl.when(jnp.logical_not(mine))
    def _():
        pltpu.make_async_copy(send_c.at[0], send_c.at[0], own_sem).wait()

    modes = recv_c.reshape(128, 128)[...]
    for h in range(2):
        mixed = stage_mix(
            modes[h * 64 : h * 64 + 64],
            spread,
            fold[...],
            lambda r, p, q, lane: weight[r, p, 2 * h + q, :, lane : lane + 128],
        )
        send_d.reshape(128, 128)[h * 64 : h * 64 + 64] = mixed.astype(BF)

    home = 2 * aisle
    own = (row - home) * 16 + aisle

    @pl.loop(0, 32)
    def _(i):
        h = i // 16
        to = i % 16
        target_row = home + h
        same = jnp.logical_and(target_row == row, to == aisle)

        @pl.when(same)
        def _():
            local(3, send_d.at[i], recv_d.at[row])

        @pl.when(jnp.logical_not(same))
        def _():
            remote(3, send_d.at[i], recv_d.at[row], (target_row, to))

    arrived(3, recv_d)
    back = dot(t3[...], recv_d.reshape(128, 128)[...])
    send_e.reshape(128, 128)[...] = back.astype(BF)

    local(4, send_e.at[:, row], recv_e.at[:, row])

    @pl.loop(1, NR)
    def _(i):
        to = lax.rem(row + i, NR)
        remote(4, send_e.at[:, to], recv_e.at[:, row], (to, aisle))

    arrived(4, recv_e)
    whole = recv_e.reshape(128, 128)[...]
    back = stage_y_back(whole[:64], whole[64:], t4[...], pltpu.roll).astype(BF)
    for r in range(2):
        send_f[:, r] = back[r * 256 : r * 256 + 256].reshape(16, 16, 128)

    local(5, send_f.at[aisle], recv_f.at[aisle])

    @pl.loop(1, NA)
    def _(i):
        to = lax.rem(aisle + i, NA)
        remote(5, send_f.at[to], recv_f.at[aisle], (row, to))

    arrived(5, recv_f)
    planes = jnp.concatenate(
        [recv_f[:, 0].reshape(256, 128), recv_f[:, 1].reshape(256, 128)], 1
    )

    def store(x, o, value):
        out[x, :, o * 16 : o * 16 + 16, :] = value

    stage_z_back(
        planes, perm[...], iz, lambda x, o: plain[x, :, o * 16 : o * 16 + 16, :], store
    )

    sent(0, send_a.at[pl.ds(0, NA - 1)])
    sent(1, send_b.at[:, pl.ds(0, NR - 1)])
    sent(2, send_c.at[pl.ds(0, NR - 1)])
    sent(4, send_e.at[:, pl.ds(0, NR - 1)])
    sent(5, send_f.at[pl.ds(0, NA - 1)])

    @pl.when(mine)
    def _():
        sent(3, send_d.at[pl.ds(0, 31)])

    @pl.when(jnp.logical_not(mine))
    def _():
        sent(3, send_d)


def on_device(flow_state, mode_weight, bypass_weight, bias_term):
    vmem = pl.BlockSpec(memory_space=pltpu.VMEM)
    pair = lambda *shape: [pltpu.VMEM(shape, BF)] * 2
    return pl.pallas_call(
        kernel,
        out_shape=jax.ShapeDtypeStruct(flow_state.shape, BF),
        in_specs=[vmem] * 13,
        out_specs=vmem,
        scratch_shapes=[
            *pair(16, 16, 256),
            *pair(2, 32, 2, 128),
            *pair(32, 4, 128),
            *pair(32, 4, 128),
            *pair(2, 32, 2, 128),
            *pair(16, 2, 16, 128),
            pltpu.VMEM((2, 16, 32, 256), F32),
            pltpu.SemaphoreType.DMA((6,)),
            pltpu.SemaphoreType.DMA((6,)),
            pltpu.SemaphoreType.DMA,
        ],
        compiler_params=pltpu.CompilerParams(
            collective_id=0, has_side_effects=True, vmem_limit_bytes=40 * 2**20
        ),
        name="fourier_layer",
    )(flow_state, mode_weight, bypass_weight, bias_term.reshape(1, C), *tables())


def solution(mesh):
    in_specs = (P("row", "aisle", None, None), P(None, "row", "aisle", None, None), P(), P())
    return jax.shard_map(
        on_device,
        mesh=mesh,
        in_specs=in_specs,
        out_specs=P("row", "aisle", None, None),
        check_vma=False,
    )
```

time: 402 us -> 72 us (0.18); the launches traced: 395 us -> 71.4 us
  waiting for transfers between devices: 239 us -> 0 us
  blocking collectives: 59.1 us -> 0 us
  Pallas kernels: 0 us -> 58.8 us
  starting transfers between devices: 29 us -> 0 us
  local copies, waits for them, and re-layouts: 38.4 us -> 12.6 us
  between operations: 13.9 us -> 0.02 us
  matrix products: 9.43 us -> 0 us
  other arithmetic: 6.72 us -> 0 us
    reduce_scatter x1 -> x0, waiting for transfers between devices: 213 us -> none  [on_device(): lax.psum_scatter(y_forward(cos_table, sin_table, z_real, z_imag).astype(j...]
    all_gather x1 -> x0, blocking collectives: 59.1 us -> none  [on_device(): incoming = lax.all_gather(back_x, 'aisle', axis=2, tiled=True)]
    pallas_call x0 -> x1, Pallas kernels: none -> 58.8 us  [on_device(): pl.pallas_call(kernel, out_shape=jax.ShapeDtypeStruct(flow_state.shape, B...]
    all_to_all x4 -> x0, starting transfers between devices: 29 us -> none  [the longest x1 13.4 us: on_device(): lax.all_to_all(flat_sums, 'row', split_axis=3, concat_axis=2, tiled=True)]
    all_to_all x4 -> x0, waiting for transfers between devices: 25.3 us -> none  [the longest x1 8.02 us: on_device(): lax.all_to_all(flat_mixed, 'row', split_axis=3, concat_axis=0, tiled=True)]
    dot_general x11 -> x0, matrix products: 7.08 us -> none  [the longest x8 5.16 us: contract(): return jnp.einsum(pattern, left, right, preferred_element_type=jnp.float32)]
    unnamed x2 -> x0, other arithmetic: 5.86 us -> none
    another operation x6 -> x0, local copies, waits for them, and re-layouts: 5.71 us -> none  [the longest x1 3.91 us: y_forward(): return jnp.stack([out_real, out_imag], 1)]
  transfers between devices with their start and end apart: 5 -> 0, of which waited for: 5 -> 0; matrix products, arithmetic and copies ran while one was open for 2% -> 0% of each run, Pallas kernels for 0% -> 0%
where the time goes in v1:
time: 72 us; the launch traced here: 71.4 us
  Pallas kernels  58.8 us (82%)
  local copies, waits for them, and re-layouts  12.6 us (18%)
    pallas_call x1, Pallas kernels, on_device(): pl.pallas_call(kernel, out_shape=jax.ShapeDtypeStruct(flow_state.shape, B...  58.8 us
    unnamed x27, local copies, waits for them, and re-layouts  12.6 us

profile of v1, /device:TPU:1, one launch (start us, length us, event | category | flops | bytes accessed | tf_op | source)
XLA Modules:
  0.0 71.4 jit_solution(2495618124237561027)
XLA Ops:
  0.0 0.0 copy-start.12
  0.0 0.7 copy-done.12
  0.7 0.0 copy-start
  0.7 1.2 %copy-done = bf16[2,2,4,32,1024]{4,3,2,1,0:T(8,128)(2,1)S(1)} copy-done((bf16[2,2,4,32,1024]{4,3,2,1,0:T(8,128)(2,1)S(1)}, bf16[2,2,4,32,1024]{4,3,2,1,0:T(8,128)(2,1)}, u32[]{:S(2)}) %copy-start) | copy-done | bytes 1048600
  1.9 0.0 copy-start.1
  1.9 1.0 %copy-done.1 = bf16[2,16,32,256]{3,2,1,0:T(8,128)(2,1)S(1)} copy-done((bf16[2,16,32,256]{3,2,1,0:T(8,128)(2,1)S(1)}, bf16[2,16,32,256]{3,2,1,0:T(8,128)(2,1)}, u32[]{:S(2)}) %copy-start.1) | copy-done | bytes 524312
  2.9 0.0 copy-start.2
  2.9 1.0 %copy-done.2 = bf16[4,256,256]{2,1,0:T(8,128)(2,1)S(1)} copy-done((bf16[4,256,256]{2,1,0:T(8,128)(2,1)S(1)}, bf16[4,256,256]{2,1,0:T(8,128)(2,1)}, u32[]{:S(2)}) %copy-start.2) | copy-done | bytes 524312
  4.0 0.0 copy-start.3
  4.0 1.0 %copy-done.3 = bf16[4,256,256]{2,1,0:T(8,128)(2,1)S(1)} copy-done((bf16[4,256,256]{2,1,0:T(8,128)(2,1)S(1)}, bf16[4,256,256]{2,1,0:T(8,128)(2,1)}, u32[]{:S(2)}) %copy-start.3) | copy-done | bytes 524312
  5.0 0.0 copy-start.4
  5.0 0.9 %copy-done.4 = bf16[64,2048]{1,0:T(8,128)(2,1)S(1)} copy-done((bf16[64,2048]{1,0:T(8,128)(2,1)S(1)}, bf16[64,2048]{1,0:T(8,128)(2,1)}, u32[]{:S(2)}) %copy-start.4) | copy-done | bytes 262168
  6.0 0.0 copy-start.5
  6.0 0.9 %copy-done.5 = bf16[512,128]{1,0:T(8,128)(2,1)S(1)} copy-done((bf16[512,128]{1,0:T(8,128)(2,1)S(1)}, bf16[512,128]{1,0:T(8,128)(2,1)}, u32[]{:S(2)}) %copy-start.5) | copy-done | bytes 131096
  6.9 0.0 copy-start.6
  6.9 0.9 %copy-done.6 = bf16[128,512]{1,0:T(8,128)(2,1)S(1)} copy-done((bf16[128,512]{1,0:T(8,128)(2,1)S(1)}, bf16[128,512]{1,0:T(8,128)(2,1)}, u32[]{:S(2)}) %copy-start.6) | copy-done | bytes 131096
  7.8 0.0 copy-start.7
  7.8 0.9 %copy-done.7 = bf16[128,512]{1,0:T(8,128)(2,1)S(1)} copy-done((bf16[128,512]{1,0:T(8,128)(2,1)S(1)}, bf16[128,512]{1,0:T(8,128)(2,1)}, u32[]{:S(2)}) %copy-start.7) | copy-done | bytes 131096
  8.7 0.9 %copy-done.8 = bf16[256,256]{1,0:T(8,128)(2,1)S(1)} copy-done((bf16[256,256]{1,0:T(8,128)(2,1)S(1)}, bf16[256,256]{1,0:T(8,128)(2,1)}, u32[]{:S(2)}) %copy-start.8) | copy-done | bytes 131096
  9.6 0.8 %copy-done.9 = bf16[128,128]{1,0:T(8,128)(2,1)S(1)} copy-done((bf16[128,128]{1,0:T(8,128)(2,1)S(1)}, bf16[128,128]{1,0:T(8,128)(2,1)}, u32[]{:S(2)}) %copy-start.9) | copy-done | bytes 32792
  10.3 0.8 %copy-done.10 = bf16[128,128]{1,0:T(8,128)(2,1)S(1)} copy-done((bf16[128,128]{1,0:T(8,128)(2,1)S(1)}, bf16[128,128]{1,0:T(8,128)(2,1)}, u32[]{:S(2)}) %copy-start.10) | copy-done | bytes 32792
  11.1 0.7 copy-done.11
  11.8 58.8 %fourier_layer.1 = bf16[2,16,32,256]{3,2,1,0:T(8,128)(2,1)S(1)} custom-call(bf16[2,16,32,256]{3,2,1,0:T(8,128)(2,1)S(1)} %copy-done.1, bf16[2,2,4,32,1024]{4,3,2,1,0:T(8,128)(2,1)S(1)} %copy-done, bf16[32,32]{1,0:T(8,128)(2,1)S(1)} %copy-done.11, f32[1,32]{1,0:T(1,128)S(1)} %bitcast.1, bf16[4,256,256]{2,1,0:T(8,128)(2,1)S(1)} %copy-done.3, ...), custom_call_target="tpu_custom_call" | custom-call | tf_op jit(solution)/shard_map/fourier_layer/pallas_call | solution.py:333
  70.6 0.8 %copy.15 = bf16[2,16,32,256]{3,2,1,0:T(8,128)(2,1)} copy(bf16[2,16,32,256]{3,2,1,0:T(8,128)(2,1)S(1)} %fourier_layer.1) | data formatting | bytes 1048576
  (4 shorter events, 0.0 us)
Async XLA Ops:
  0.0 0.7 copy-start.12
  0.7 1.2 %copy-start = (bf16[2,2,4,32,1024]{4,3,2,1,0:T(8,128)(2,1)S(1)}, bf16[2,2,4,32,1024]{4,3,2,1,0:T(8,128)(2,1)}, u32[]{:S(2)}) copy-start(bf16[2,2,4,32,1024]{4,3,2,1,0:T(8,128)(2,1)} %weight.1) | copy-start | bytes 3145732
  1.9 1.0 %copy-start.1 = (bf16[2,16,32,256]{3,2,1,0:T(8,128)(2,1)S(1)}, bf16[2,16,32,256]{3,2,1,0:T(8,128)(2,1)}, u32[]{:S(2)}) copy-start(bf16[2,16,32,256]{3,2,1,0:T(8,128)(2,1)} %flow.1) | copy-start | bytes 1572868
  2.9 1.0 %copy-start.2 = (bf16[4,256,256]{2,1,0:T(8,128)(2,1)S(1)}, bf16[4,256,256]{2,1,0:T(8,128)(2,1)}, u32[]{:S(2)}) copy-start(bf16[4,256,256]{2,1,0:T(8,128)(2,1)} %constant.26.clone.iz) | copy-start | bytes 1572868
  4.0 1.0 %copy-start.3 = (bf16[4,256,256]{2,1,0:T(8,128)(2,1)S(1)}, bf16[4,256,256]{2,1,0:T(8,128)(2,1)}, u32[]{:S(2)}) copy-start(bf16[4,256,256]{2,1,0:T(8,128)(2,1)} %constant.18.clone.fz) | copy-start | bytes 1572868
  5.0 0.9 %copy-start.4 = (bf16[64,2048]{1,0:T(8,128)(2,1)S(1)}, bf16[64,2048]{1,0:T(8,128)(2,1)}, u32[]{:S(2)}) copy-start(bf16[64,2048]{1,0:T(8,128)(2,1)} %constant.22.clone.spread) | copy-start | bytes 786436
  6.0 0.9 %copy-start.5 = (bf16[512,128]{1,0:T(8,128)(2,1)S(1)}, bf16[512,128]{1,0:T(8,128)(2,1)}, u32[]{:S(2)}) copy-start(bf16[512,128]{1,0:T(8,128)(2,1)} %constant.25.clone.t4) | copy-start | bytes 393220
  6.9 0.9 %copy-start.6 = (bf16[128,512]{1,0:T(8,128)(2,1)S(1)}, bf16[128,512]{1,0:T(8,128)(2,1)}, u32[]{:S(2)}) copy-start(bf16[128,512]{1,0:T(8,128)(2,1)} %constant.23.clone.fold) | copy-start | bytes 393220
  7.8 0.9 %copy-start.7 = (bf16[128,512]{1,0:T(8,128)(2,1)S(1)}, bf16[128,512]{1,0:T(8,128)(2,1)}, u32[]{:S(2)}) copy-start(bf16[128,512]{1,0:T(8,128)(2,1)} %constant.20.clone.t1) | copy-start | bytes 393220
  8.7 0.9 %copy-start.8 = (bf16[256,256]{1,0:T(8,128)(2,1)S(1)}, bf16[256,256]{1,0:T(8,128)(2,1)}, u32[]{:S(2)}) copy-start(bf16[256,256]{1,0:T(8,128)(2,1)} %constant.19.clone.perm) | copy-start | bytes 393220
  9.6 0.8 %copy-start.9 = (bf16[128,128]{1,0:T(8,128)(2,1)S(1)}, bf16[128,128]{1,0:T(8,128)(2,1)}, u32[]{:S(2)}) copy-start(bf16[128,128]{1,0:T(8,128)(2,1)} %constant.24.clone.t3) | copy-start | bytes 98308
  10.3 0.8 %copy-start.10 = (bf16[128,128]{1,0:T(8,128)(2,1)S(1)}, bf16[128,128]{1,0:T(8,128)(2,1)}, u32[]{:S(2)}) copy-start(bf16[128,128]{1,0:T(8,128)(2,1)} %constant.21.clone.t2) | copy-start | bytes 98308
  11.1 0.7 copy-start.11

commit v2 on v1

--- a/solution.py
+++ b/solution.py
@@ -46,17 +46,42 @@
     perm = np.einsum("ab,cd->acdb", eye, eye).reshape(256, 256)
     cy, sy = twiddle(np.arange(MY) - MY // 2, np.arange(NY), NY)
     ty = np.stack([np.stack([cy, sy]), np.stack([-sy, cy])])
-    t1 = ty.reshape(2, 2, 32, 2, NY).transpose(3, 2, 0, 1, 4).reshape(128, 512)
+    t1 = ty.reshape(2, 2, 32, 2, 2, 128).transpose(4, 3, 2, 0, 1, 5).reshape(256, 256)
     cx, sx = twiddle(np.arange(MX) - MX // 2, np.arange(NX), NX)
     tx = np.stack([np.stack([cx, sx]), np.stack([-sx, cx])])
     t2 = tx.reshape(2, 2, MX, 32, 2).transpose(2, 0, 4, 3, 1).reshape(128, 128)
     bx = np.stack([np.stack([cx, -sx]), np.stack([sx, cx])])
     t3 = bx.reshape(2, 2, MX, 32, 2).transpose(4, 3, 0, 2, 1).reshape(128, 128)
     by = np.stack([np.stack([cy, -sy]), np.stack([sy, cy])])
-    t4 = by.reshape(2, 2, 32, 2, NY).transpose(0, 4, 3, 2, 1).reshape(512, 128)
-    spread = np.einsum("ab,cd,o->acdbo", eye, np.eye(4), np.ones(32)).reshape(64, 2048)
-    fold = np.einsum("lm,ab,cd,g->lacdgmb", np.eye(2), eye, np.eye(4), np.ones(4)).reshape(128, 512)
-    return [jnp.asarray(t, BF) for t in (fz, perm, t1, t2, spread, fold, t3, t4, iz)]
+    t4 = by.reshape(2, 2, 32, 2, 2, 128).transpose(0, 5, 4, 3, 2, 1).reshape(256, 256)
+    spread = np.einsum("ab,ij,cd,o->iacdbjo", np.eye(8), np.eye(2), np.eye(4), np.ones(32))
+    spread = spread.reshape(64, 2048)
+    fold = np.einsum("lm,ab,ij,cd,g->liacdgmbj", np.eye(2), np.eye(8), np.eye(2), np.eye(4), np.ones(4))
+    fold = fold.reshape(128, 512)
+    halves = lambda t: np.concatenate(np.split(t, t.shape[1] // 256, 1), 0)
+    packed = [
+        fz.reshape(1024, 256),
+        perm,
+        t1,
+        np.concatenate([t2, t3], 1),
+        halves(spread),
+        halves(fold),
+        t4,
+        iz.reshape(1024, 256),
+    ]
+    return jnp.asarray(np.concatenate(packed, 0), BF)
+
+
+FZ = 0
+PERM = 1024
+T1 = 1280
+T23 = 1536
+SPREAD = 1664
+FOLD = 2176
+T4 = 2432
+IZ = 2688
+ROWS = 3712
+GROUPS = ((FZ, T1), (T1, SPREAD), (SPREAD, T4), (T4, ROWS))
 
 
 def dot(left, right):
@@ -88,9 +113,31 @@
     return dot(perm, total.astype(BF)).astype(BF)
 
 
+def near(place, index):
+    return ((index - place + 10) & 7) < 4
+
+
+def near_tables(place, t1, t4):
+    columns = (lax.broadcasted_iota(jnp.int32, (128, 256), 1) >> 5) & 3
+    rows = (lax.broadcasted_iota(jnp.int32, (256, 128), 0) >> 5) & 3
+    first, second = t1[:128].astype(F32), t1[128:].astype(F32)
+    left, right = t4[:, :128].astype(F32), t4[:, 128:].astype(F32)
+    return (
+        jnp.where(near(place, columns), first, second).astype(BF),
+        jnp.where(near(place, rows), left, right).astype(BF),
+    )
+
+
 def stage_y(gathered, t1, roll):
-    sums = dot(t1, jnp.concatenate([gathered[:, :128], gathered[:, 128:]], 0))
-    return exchange_halves(sums[:64], sums[64:], roll)
+    wide = jnp.concatenate(gathered, 1)
+    upper = jnp.concatenate([wide[:, 0:128], wide[:, 256:384]], 1)
+    lower = jnp.concatenate([wide[:, 128:256], wide[:, 384:512]], 1)
+    sums = dot(t1, jnp.concatenate([upper, lower], 0))
+    parts = [
+        exchange_halves(sums[:64, c * 128 : c * 128 + 128], sums[64:, c * 128 : c * 128 + 128], roll)
+        for c in range(2)
+    ]
+    return [parts[c][x] for x in range(2) for c in range(2)]
 
 
 def stage_mix(modes, spread, fold, weight):
@@ -119,9 +166,12 @@
     return jnp.concatenate([mixed[:64], mixed[64:]], 1)
 
 
-def stage_y_back(first, second, t4, roll):
-    low, high = exchange_halves(first.astype(F32), second.astype(F32), roll)
-    return dot(t4, jnp.concatenate([low, high], 0).astype(BF))
+def stage_y_back(parts, t4, roll):
+    columns = []
+    for o in range(2):
+        low, high = exchange_halves(parts[o].astype(F32), parts[2 + o].astype(F32), roll)
+        columns.append(jnp.concatenate([low, high], 0).astype(BF))
+    return dot(t4, jnp.concatenate(columns, 1))
 
 
 def bypass_matrix(bypass, lanes):
@@ -141,28 +191,53 @@
             store(x, o, jax.nn.gelu(total).astype(BF))
 
 
-def kernel(
-    flow, weight, bypass, bias, fz, perm, t1, t2, spread, fold, t3, t4, iz,
+def stages(
+    flow_hbm, weight_hbm, bypass_hbm, bias_hbm, table_hbm,
     out,
+    flow, weight, bypass, bias, table,
     send_a, recv_a, send_b, recv_b, send_c, recv_c, send_d, recv_d, send_e, recv_e, send_f, recv_f,
-    plain, send_sem, recv_sem, own_sem,
+    plain, send_sem, recv_sem, own_sem, load_sem, ending,
 ):
     row = lax.axis_index("row")
     aisle = lax.axis_index("aisle")
     quad = row // 2
     half = row % 2
+    place = aisle // 2
+    side = aisle % 2
+    group = aisle % 8
+
+    loads = [pltpu.make_async_copy(flow_hbm, flow, load_sem.at[0])]
+    for i, (first, last) in enumerate(GROUPS):
+        part = pl.ds(first, last - first)
+        loads.append(pltpu.make_async_copy(table_hbm.at[part], table.at[part], load_sem.at[i + 1]))
+    loads.append(pltpu.make_async_copy(bypass_hbm, bypass, load_sem.at[5]))
+    loads.append(pltpu.make_async_copy(bias_hbm, bias, load_sem.at[6]))
+    loads.append(pltpu.make_async_copy(weight_hbm, weight, load_sem.at[7]))
+    for load in loads:
+        load.start()
+
     barrier = pltpu.get_barrier_semaphore()
 
-    @pl.loop(1, NA)
-    def _(i):
-        pl.semaphore_signal(barrier, inc=1, device_id=(row, lax.rem(aisle + i, NA)), device_id_type=MESH)
+    @pl.loop(0, 10)
+    def _(i):
+        other = ((place + i // 2 + 5) % 8) * 2 + i % 2
+
+        @pl.when(other != aisle)
+        def _():
+            pl.semaphore_signal(barrier, inc=1, device_id=(row, other), device_id_type=MESH)
 
     @pl.loop(1, NR)
     def _(i):
         pl.semaphore_signal(barrier, inc=1, device_id=(lax.rem(row + i, NR), aisle), device_id_type=MESH)
 
-    send_a[...] = stage_z(flow, fz, perm[...]).reshape(16, 16, 256)
-    pl.semaphore_wait(barrier, NA - 1 + NR - 1)
+    def tile(first, rows=256):
+        return table[first : first + rows]
+
+    loads[0].wait()
+    loads[1].wait()
+    fz = [tile(FZ + 256 * i) for i in range(4)]
+    send_a[...] = stage_z(flow, fz, tile(PERM)).reshape(8, 2, 16, 256)
+    pl.semaphore_wait(barrier, 9 + NR - 1)
 
     def remote(stage, source, target, device):
         pltpu.make_async_remote_copy(
@@ -183,13 +258,20 @@
     def sent(stage, part):
         pltpu.make_async_copy(part, part, send_sem.at[stage]).wait()
 
-    local(0, send_a.at[aisle], recv_a.at[aisle])
-
-    @pl.loop(1, NA)
-    def _(i):
-        to = lax.rem(aisle + i, NA)
-        remote(0, send_a.at[to], recv_a.at[aisle], (row, to))
-
+    local(0, send_a.at[group], recv_a.at[group])
+
+    @pl.loop(0, 8)
+    def _(i):
+        to = ((place + 7 + i // 2) % 8) * 2 + i % 2
+
+        @pl.when(to != aisle)
+        def _():
+            remote(0, send_a.at[to % 8], recv_a.at[group], (row, to))
+
+    ending.append(lambda: sent(0, send_a.at[pl.ds(0, 7)]))
+
+    loads[5].wait()
+    loads[6].wait()
     lanes = (
         lax.broadcasted_iota(jnp.int32, (32, 256), 0)
         == lax.broadcasted_iota(jnp.int32, (32, 256), 1) % 32
@@ -203,10 +285,14 @@
             field = flow[x, y * 8 : y * 8 + 8].reshape(256, 256)
             plain[x, y * 8 : y * 8 + 8] = (dot_tn(diagonal, field) + tall).reshape(8, 32, 256)
 
+    for i in (2, 3, 4, 7):
+        loads[i].wait()
+    t1, t4 = near_tables(place, tile(T1), tile(T4))
     arrived(0, recv_a)
-    first, second = stage_y(recv_a[...].reshape(256, 256), t1[...], pltpu.roll)
-    send_b.reshape(128, 128)[:64] = first.astype(BF)
-    send_b.reshape(128, 128)[64:] = second.astype(BF)
+    yield
+    parts = stage_y([recv_a[:, c].reshape(128, 256) for c in range(2)], t1, pltpu.roll)
+    for i in range(4):
+        send_b.reshape(256, 128)[i * 64 : i * 64 + 64] = parts[i].astype(BF)
 
     local(1, send_b.at[:, row], recv_b.at[:, row])
 
@@ -215,22 +301,27 @@
         to = lax.rem(row + i, NR)
         remote(1, send_b.at[:, to], recv_b.at[:, row], (to, aisle))
 
+    ending.append(lambda: sent(1, send_b.at[:, pl.ds(0, NR - 1)]))
     arrived(1, recv_b)
-    modes = dot(t2[...], recv_b.reshape(128, 128)[...]) * SCALING
-    send_c.reshape(128, 128)[...] = modes.astype(BF)
+    yield
+    whole = recv_b.reshape(256, 128)[...]
+    columns = [jnp.concatenate([whole[c * 64 : c * 64 + 64], whole[128 + c * 64 : 192 + c * 64]], 0) for c in range(2)]
+    modes = (dot(tile(T23, 128)[:, :128], jnp.concatenate(columns, 1)) * SCALING).astype(BF)
+    for c in range(2):
+        send_c.reshape(256, 128)[c * 128 : c * 128 + 128] = modes[:, c * 128 : c * 128 + 128]
 
     mine = quad == aisle
     slot = half * 16 + aisle
 
     @pl.when(mine)
     def _():
-        local(2, send_c.at[row], recv_c.at[slot])
+        local(2, send_c.at[:, row], recv_c.at[:, slot])
 
     @pl.when(jnp.logical_not(mine))
     def _():
         pltpu.make_async_remote_copy(
-            src_ref=send_c.at[row],
-            dst_ref=recv_c.at[slot],
+            src_ref=send_c.at[:, row],
+            dst_ref=recv_c.at[:, slot],
             send_sem=own_sem,
             recv_sem=recv_sem.at[2],
             device_id=(row, quad),
@@ -240,26 +331,35 @@
     @pl.loop(1, NR)
     def _(i):
         to = lax.rem(row + i, NR)
-        remote(2, send_c.at[to], recv_c.at[slot], (to, quad))
+        remote(2, send_c.at[:, to], recv_c.at[:, slot], (to, quad))
+
+    ending.append(lambda: sent(2, send_c.at[:, pl.ds(0, NR - 1)]))
+    @ending.append
+    def _():
+        @pl.when(jnp.logical_not(mine))
+        def _():
+            pltpu.make_async_copy(send_c.at[:, 0], send_c.at[:, 0], own_sem).wait()
 
     arrived(2, recv_c)
-
-    @pl.when(jnp.logical_not(mine))
-    def _():
-        pltpu.make_async_copy(send_c.at[0], send_c.at[0], own_sem).wait()
-
-    modes = recv_c.reshape(128, 128)[...]
+    yield
+
+    spread = jnp.concatenate([tile(SPREAD + 64 * i, 64) for i in range(8)], 1)
+    fold = jnp.concatenate([tile(FOLD, 128), tile(FOLD + 128, 128)], 1)
+    whole = recv_c.reshape(256, 128)[...]
     for h in range(2):
+        modes = []
+        for c in range(2):
+            first = c * 128 + h * 64
+            modes.append(whole[first : first + 32].astype(F32) + whole[first + 32 : first + 64].astype(F32))
         mixed = stage_mix(
-            modes[h * 64 : h * 64 + 64],
+            jnp.concatenate(modes, 0).astype(BF),
             spread,
-            fold[...],
+            fold,
             lambda r, p, q, lane: weight[r, p, 2 * h + q, :, lane : lane + 128],
         )
         send_d.reshape(128, 128)[h * 64 : h * 64 + 64] = mixed.astype(BF)
 
     home = 2 * aisle
-    own = (row - home) * 16 + aisle
 
     @pl.loop(0, 32)
     def _(i):
@@ -270,15 +370,30 @@
 
         @pl.when(same)
         def _():
-            local(3, send_d.at[i], recv_d.at[row])
+            local(3, send_d.at[h, :, to % 8], recv_d.at[:, row])
 
         @pl.when(jnp.logical_not(same))
         def _():
-            remote(3, send_d.at[i], recv_d.at[row], (target_row, to))
+            remote(3, send_d.at[h, :, to % 8], recv_d.at[:, row], (target_row, to))
+
+    @ending.append
+    def _():
+        @pl.when(mine)
+        def _():
+            sent(3, recv_d.at[:, pl.ds(0, 31)])
+
+        @pl.when(jnp.logical_not(mine))
+        def _():
+            sent(3, recv_d)
 
     arrived(3, recv_d)
-    back = dot(t3[...], recv_d.reshape(128, 128)[...])
-    send_e.reshape(128, 128)[...] = back.astype(BF)
+    yield
+    whole = recv_d.reshape(256, 128)[...]
+    back = dot(tile(T23, 128)[:, 128:], jnp.concatenate([whole[:128], whole[128:]], 1)).astype(BF)
+    for x in range(2):
+        for o in range(2):
+            i = 2 * x + o
+            send_e.reshape(256, 128)[i * 64 : i * 64 + 64] = back[x * 64 : x * 64 + 64, o * 128 : o * 128 + 128]
 
     local(4, send_e.at[:, row], recv_e.at[:, row])
 
@@ -287,71 +402,84 @@
         to = lax.rem(row + i, NR)
         remote(4, send_e.at[:, to], recv_e.at[:, row], (to, aisle))
 
+    ending.append(lambda: sent(4, send_e.at[:, pl.ds(0, NR - 1)]))
     arrived(4, recv_e)
-    whole = recv_e.reshape(128, 128)[...]
-    back = stage_y_back(whole[:64], whole[64:], t4[...], pltpu.roll).astype(BF)
+    yield
+    whole = recv_e.reshape(256, 128)[...]
+    back = stage_y_back([whole[i * 64 : i * 64 + 64] for i in range(4)], t4, pltpu.roll).astype(BF)
     for r in range(2):
-        send_f[:, r] = back[r * 256 : r * 256 + 256].reshape(16, 16, 128)
-
-    local(5, send_f.at[aisle], recv_f.at[aisle])
-
-    @pl.loop(1, NA)
-    def _(i):
-        to = lax.rem(aisle + i, NA)
-        remote(5, send_f.at[to], recv_f.at[aisle], (row, to))
-
+        for o in range(2):
+            part = back[r * 128 : r * 128 + 128, o * 128 : o * 128 + 128]
+            send_f[:, r, o] = part.reshape(8, 16, 128)
+
+    local(5, send_f.at[group], recv_f.at[group])
+
+    @pl.loop(0, 8)
+    def _(i):
+        to = ((place + 6 + i // 2) % 8) * 2 + i % 2
+
+        @pl.when(to != aisle)
+        def _():
+            remote(5, send_f.at[to % 8], recv_f.at[group], (row, to))
+
+    ending.append(lambda: sent(5, send_f.at[pl.ds(0, 7)]))
     arrived(5, recv_f)
+    yield
     planes = jnp.concatenate(
         [recv_f[:, 0].reshape(256, 128), recv_f[:, 1].reshape(256, 128)], 1
     )
 
+    iz = [tile(IZ + 256 * i) for i in range(4)]
+
     def store(x, o, value):
         out[x, :, o * 16 : o * 16 + 16, :] = value
 
     stage_z_back(
-        planes, perm[...], iz, lambda x, o: plain[x, :, o * 16 : o * 16 + 16, :], store
+        planes, tile(PERM), iz, lambda x, o: plain[x, :, o * 16 : o * 16 + 16, :], store
     )
-
-    sent(0, send_a.at[pl.ds(0, NA - 1)])
-    sent(1, send_b.at[:, pl.ds(0, NR - 1)])
-    sent(2, send_c.at[pl.ds(0, NR - 1)])
-    sent(4, send_e.at[:, pl.ds(0, NR - 1)])
-    sent(5, send_f.at[pl.ds(0, NA - 1)])
-
-    @pl.when(mine)
-    def _():
-        sent(3, send_d.at[pl.ds(0, 31)])
-
-    @pl.when(jnp.logical_not(mine))
-    def _():
-        sent(3, send_d)
+    yield
+
+
+def kernel(*refs):
+    ending = []
+    for _ in stages(*refs, ending):
+        pass
+    for wait in ending:
+        wait()
 
 
 def on_device(flow_state, mode_weight, bypass_weight, bias_term):
-    vmem = pl.BlockSpec(memory_space=pltpu.VMEM)
+    hbm = pl.BlockSpec(memory_space=pltpu.HBM)
     pair = lambda *shape: [pltpu.VMEM(shape, BF)] * 2
     return pl.pallas_call(
         kernel,
         out_shape=jax.ShapeDtypeStruct(flow_state.shape, BF),
-        in_specs=[vmem] * 13,
-        out_specs=vmem,
+        in_specs=[hbm] * 5,
+        out_specs=pl.BlockSpec(memory_space=pltpu.VMEM),
         scratch_shapes=[
-            *pair(16, 16, 256),
-            *pair(2, 32, 2, 128),
-            *pair(32, 4, 128),
-            *pair(32, 4, 128),
-            *pair(2, 32, 2, 128),
-            *pair(16, 2, 16, 128),
+            pltpu.VMEM(flow_state.shape, BF),
+            pltpu.VMEM(mode_weight.shape, BF),
+            pltpu.VMEM(bypass_weight.shape, BF),
+            pltpu.VMEM((1, C), F32),
+            pltpu.VMEM((ROWS, 256), BF),
+            *pair(8, 2, 16, 256),
+            *pair(4, 32, 2, 128),
+            *pair(2, 32, 4, 128),
+            pltpu.VMEM((2, 2, 8, 4, 128), BF),
+            pltpu.VMEM((2, 32, 4, 128), BF),
+            *pair(4, 32, 2, 128),
+            *pair(8, 2, 2, 16, 128),
             pltpu.VMEM((2, 16, 32, 256), F32),
             pltpu.SemaphoreType.DMA((6,)),
             pltpu.SemaphoreType.DMA((6,)),
             pltpu.SemaphoreType.DMA,
+            pltpu.SemaphoreType.DMA((8,)),
         ],
         compiler_params=pltpu.CompilerParams(
-            collective_id=0, has_side_effects=True, vmem_limit_bytes=40 * 2**20
+            collective_id=0, has_side_effects=True, vmem_limit_bytes=60 * 2**20
         ),
         name="fourier_layer",
-    )(flow_state, mode_weight, bypass_weight, bias_term.reshape(1, C), *tables())
+    )(flow_state, mode_weight, bypass_weight, bias_term.reshape(1, C), tables())
 
 
 def solution(mesh):

time: 72 us -> 62.4 us (0.87)
  local copies, waits for them, and re-layouts: 12.6 us -> 1.87 us
  Pallas kernels: 58.8 us -> 60.4 us
    unnamed x27 -> x1, local copies, waits for them, and re-layouts: 12.6 us -> 1.87 us
    pallas_call x1, Pallas kernels: 58.8 us -> 60.4 us  [on_device(): pl.pallas_call(kernel, out_shape=jax.ShapeDtypeStruct(flow_state.shape, B...]
where the time goes in v2:
time: 62.4 us; the launch traced here: 62.2 us
  Pallas kernels  60.4 us (97%)
  local copies, waits for them, and re-layouts  1.87 us (3%)
    pallas_call x1, Pallas kernels, on_device(): pl.pallas_call(kernel, out_shape=jax.ShapeDtypeStruct(flow_state.shape, B...  60.4 us
    unnamed x1, local copies, waits for them, and re-layouts  1.87 us

profile of v2, /device:TPU:1, one launch (start us, length us, event | category | flops | bytes accessed | tf_op | source)
XLA Modules:
  0.0 62.2 jit_solution(13646394106601138672)
XLA Ops:
  0.0 60.4 %fourier_layer.1 = bf16[2,16,32,256]{3,2,1,0:T(8,128)(2,1)} custom-call(bf16[2,16,32,256]{3,2,1,0:T(8,128)(2,1)} %refs_0_.1, bf16[2,2,4,32,1024]{4,3,2,1,0:T(8,128)(2,1)} %refs_1_.1, bf16[32,32]{1,0:T(8,128)(2,1)} %refs_2_.1, f32[1,32]{1,0:T(1,128)} %bitcast.1, bf16[3712,256]{1,0:T(8,128)(2,1)} %constant.2.clone.refs_4_), custom_call_target="tpu_custom_call" | custom-call | tf_op jit(solution)/shard_map/fourier_layer/pallas_call | solution.py:454
  60.4 1.9 %copy.7 = bf16[2,16,32,256]{3,2,1,0:T(8,128)(2,1)} copy(bf16[2,16,32,256]{3,2,1,0:T(8,128)(2,1)} %fourier_layer.1) | data formatting | bytes 1048576

commit v3 on v2

--- a/solution.py
+++ b/solution.py
@@ -200,7 +200,8 @@
 ):
     row = lax.axis_index("row")
     aisle = lax.axis_index("aisle")
-    quad = row // 2
+    held = (row - 2 * aisle + NR) % NR
+    quad = held // 2
     half = row % 2
     place = aisle // 2
     side = aisle % 2
@@ -218,17 +219,25 @@
 
     barrier = pltpu.get_barrier_semaphore()
 
-    @pl.loop(0, 10)
+    def away(i):
+        return (12 + (i + 1) // 2 * (1 - 2 * (i % 2))) % 8
+
+    def row_at(i):
+        low = (row // 16 + 1 - i % 4 // 2) % 2
+        return low * 16 + (row // 2 + away(i // 4)) % 8 * 2 + (row + 1 - i % 2) % 2
+
+    def aisle_at(step, other):
+        return (place + step + 8) % 8 * 2 + (side + other) % 2
+
+    for step in (-3, -2, -1, 1, 0):
+        for other in (1, 0):
+            if step or other:
+                to = aisle_at(step, other)
+                pl.semaphore_signal(barrier, inc=1, device_id=(row, to), device_id_type=MESH)
+
+    @pl.loop(0, NR - 1)
     def _(i):
-        other = ((place + i // 2 + 5) % 8) * 2 + i % 2
-
-        @pl.when(other != aisle)
-        def _():
-            pl.semaphore_signal(barrier, inc=1, device_id=(row, other), device_id_type=MESH)
-
-    @pl.loop(1, NR)
-    def _(i):
-        pl.semaphore_signal(barrier, inc=1, device_id=(lax.rem(row + i, NR), aisle), device_id_type=MESH)
+        pl.semaphore_signal(barrier, inc=1, device_id=(row_at(i), aisle), device_id_type=MESH)
 
     def tile(first, rows=256):
         return table[first : first + rows]
@@ -258,15 +267,12 @@
     def sent(stage, part):
         pltpu.make_async_copy(part, part, send_sem.at[stage]).wait()
 
+    for step in (2, -1, 1, 0):
+        for other in (1, 0):
+            to = aisle_at(step, other)
+            if step or other:
+                remote(0, send_a.at[to % 8], recv_a.at[group], (row, to))
     local(0, send_a.at[group], recv_a.at[group])
-
-    @pl.loop(0, 8)
-    def _(i):
-        to = ((place + 7 + i // 2) % 8) * 2 + i % 2
-
-        @pl.when(to != aisle)
-        def _():
-            remote(0, send_a.at[to % 8], recv_a.at[group], (row, to))
 
     ending.append(lambda: sent(0, send_a.at[pl.ds(0, 7)]))
 
@@ -294,12 +300,13 @@
     for i in range(4):
         send_b.reshape(256, 128)[i * 64 : i * 64 + 64] = parts[i].astype(BF)
 
-    local(1, send_b.at[:, row], recv_b.at[:, row])
-
-    @pl.loop(1, NR)
+    @pl.loop(0, NR - 1)
     def _(i):
-        to = lax.rem(row + i, NR)
-        remote(1, send_b.at[:, to], recv_b.at[:, row], (to, aisle))
+        to = row_at(i)
+        pair = (to - 2 * aisle + NR) % NR
+        remote(1, send_b.at[:, pair], recv_b.at[:, row], (to, aisle))
+
+    local(1, send_b.at[:, held], recv_b.at[:, row])
 
     ending.append(lambda: sent(1, send_b.at[:, pl.ds(0, NR - 1)]))
     arrived(1, recv_b)
@@ -312,6 +319,11 @@
 
     mine = quad == aisle
     slot = half * 16 + aisle
+
+    @pl.loop(0, NR - 1)
+    def _(i):
+        to = row_at(i)
+        remote(2, send_c.at[:, to], recv_c.at[:, slot], (to, quad))
 
     @pl.when(mine)
     def _():
@@ -327,11 +339,6 @@
             device_id=(row, quad),
             device_id_type=MESH,
         ).start()
-
-    @pl.loop(1, NR)
-    def _(i):
-        to = lax.rem(row + i, NR)
-        remote(2, send_c.at[:, to], recv_c.at[:, slot], (to, quad))
 
     ending.append(lambda: sent(2, send_c.at[:, pl.ds(0, NR - 1)]))
     @ending.append
@@ -359,13 +366,11 @@
         )
         send_d.reshape(128, 128)[h * 64 : h * 64 + 64] = mixed.astype(BF)
 
-    home = 2 * aisle
-
     @pl.loop(0, 32)
     def _(i):
-        h = i // 16
-        to = i % 16
-        target_row = home + h
+        h = i % 2
+        to = (place + away(i // 4)) % 8 * 2 + (side + 1 - i % 4 // 2) % 2
+        target_row = (aisle + to) % 16 * 2 + h
         same = jnp.logical_and(target_row == row, to == aisle)
 
         @pl.when(same)
@@ -395,12 +400,12 @@
             i = 2 * x + o
             send_e.reshape(256, 128)[i * 64 : i * 64 + 64] = back[x * 64 : x * 64 + 64, o * 128 : o * 128 + 128]
 
-    local(4, send_e.at[:, row], recv_e.at[:, row])
-
-    @pl.loop(1, NR)
+    @pl.loop(0, NR - 1)
     def _(i):
-        to = lax.rem(row + i, NR)
-        remote(4, send_e.at[:, to], recv_e.at[:, row], (to, aisle))
+        to = row_at(i)
+        remote(4, send_e.at[:, to], recv_e.at[:, held], (to, aisle))
+
+    local(4, send_e.at[:, row], recv_e.at[:, held])
 
     ending.append(lambda: sent(4, send_e.at[:, pl.ds(0, NR - 1)]))
     arrived(4, recv_e)
@@ -412,15 +417,12 @@
             part = back[r * 128 : r * 128 + 128, o * 128 : o * 128 + 128]
             send_f[:, r, o] = part.reshape(8, 16, 128)
 
+    for step in (-2, -1, 1, 0):
+        for other in (1, 0):
+            to = aisle_at(step, other)
+            if step or other:
+                remote(5, send_f.at[to % 8], recv_f.at[group], (row, to))
     local(5, send_f.at[group], recv_f.at[group])
-
-    @pl.loop(0, 8)
-    def _(i):
-        to = ((place + 6 + i // 2) % 8) * 2 + i % 2
-
-        @pl.when(to != aisle)
-        def _():
-            remote(5, send_f.at[to % 8], recv_f.at[group], (row, to))
 
     ending.append(lambda: sent(5, send_f.at[pl.ds(0, 7)]))
     arrived(5, recv_f)

time: 62.4 us -> 56.7 us (0.909)
  Pallas kernels: 60.4 us -> 54.6 us
    pallas_call x1, Pallas kernels: 60.4 us -> 54.6 us  [on_device(): pl.pallas_call(kernel, out_shape=jax.ShapeDtypeStruct(flow_state.shape, B...]
where the time goes in v3:
time: 56.7 us; the launch traced here: 56.5 us
  Pallas kernels  54.6 us (96%)
  local copies, waits for them, and re-layouts  1.87 us (3%)
    pallas_call x1, Pallas kernels, on_device(): pl.pallas_call(kernel, out_shape=jax.ShapeDtypeStruct(flow_state.shape, B...  54.6 us
    unnamed x1, local copies, waits for them, and re-layouts  1.87 us

profile of v3, /device:TPU:1, one launch (start us, length us, event | category | flops | bytes accessed | tf_op | source)
XLA Modules:
  0.0 56.5 jit_solution(17869005800099487210)
XLA Ops:
  0.0 54.6 %fourier_layer.1 = bf16[2,16,32,256]{3,2,1,0:T(8,128)(2,1)} custom-call(bf16[2,16,32,256]{3,2,1,0:T(8,128)(2,1)} %refs_0_.1, bf16[2,2,4,32,1024]{4,3,2,1,0:T(8,128)(2,1)} %refs_1_.1, bf16[32,32]{1,0:T(8,128)(2,1)} %refs_2_.1, f32[1,32]{1,0:T(1,128)} %bitcast.1, bf16[3712,256]{1,0:T(8,128)(2,1)} %constant.2.clone.refs_4_), custom_call_target="tpu_custom_call" | custom-call | tf_op jit(solution)/shard_map/fourier_layer/pallas_call | solution.py:456
  54.7 1.9 %copy.7 = bf16[2,16,32,256]{3,2,1,0:T(8,128)(2,1)} copy(bf16[2,16,32,256]{3,2,1,0:T(8,128)(2,1)} %fourier_layer.1) | data formatting | bytes 1048576

commit v4 on v3

--- a/solution.py
+++ b/solution.py
@@ -455,7 +455,7 @@
     pair = lambda *shape: [pltpu.VMEM(shape, BF)] * 2
     return pl.pallas_call(
         kernel,
-        out_shape=jax.ShapeDtypeStruct(flow_state.shape, BF),
+        out_shape=pltpu.VMEM(flow_state.shape, BF),
         in_specs=[hbm] * 5,
         out_specs=pl.BlockSpec(memory_space=pltpu.VMEM),
         scratch_shapes=[

time: 56.7 us -> 54.8 us (0.966)
  local copies, waits for them, and re-layouts: 1.87 us -> 0.8 us
  Pallas kernels: 54.6 us -> 53.9 us
    unnamed x1, local copies, waits for them, and re-layouts: 1.87 us -> 0.8 us
    pallas_call x1, Pallas kernels: 54.6 us -> 53.9 us  [on_device(): pl.pallas_call(kernel, out_shape=pltpu.VMEM(flow_state.shape, BF), in_spe...]
where the time goes in v4:
time: 54.8 us; the launch traced here: 54.7 us
  Pallas kernels  53.9 us (98%)
  local copies, waits for them, and re-layouts  0.8 us (1%)
    pallas_call x1, Pallas kernels, on_device(): pl.pallas_call(kernel, out_shape=pltpu.VMEM(flow_state.shape, BF), in_spe...  53.9 us

profile of v4, /device:TPU:1, one launch (start us, length us, event | category | flops | bytes accessed | tf_op | source)
XLA Modules:
  0.0 54.7 jit_solution(18359602042626916340)
XLA Ops:
  0.0 53.9 %fourier_layer.1 = bf16[2,16,32,256]{3,2,1,0:T(8,128)(2,1)S(1)} custom-call(bf16[2,16,32,256]{3,2,1,0:T(8,128)(2,1)} %refs_0_.1, bf16[2,2,4,32,1024]{4,3,2,1,0:T(8,128)(2,1)} %refs_1_.1, bf16[32,32]{1,0:T(8,128)(2,1)} %refs_2_.1, f32[1,32]{1,0:T(1,128)} %bitcast.1, bf16[3712,256]{1,0:T(8,128)(2,1)} %constant.2.clone.refs_4_), custom_call_target="tpu_custom_call" | custom-call | tf_op jit(solution)/shard_map/fourier_layer/pallas_call | solution.py:456
  53.9 0.8 %copy.7 = bf16[2,16,32,256]{3,2,1,0:T(8,128)(2,1)} copy(bf16[2,16,32,256]{3,2,1,0:T(8,128)(2,1)S(1)} %fourier_layer.1) | data formatting | bytes 1048576

commit v5 on v4

--- a/solution.py
+++ b/solution.py
@@ -160,9 +160,7 @@
                     imag[q] = im if imag[q] is None else imag[q] + im
         planes += [jnp.concatenate(real, 0), jnp.concatenate(imag, 0)]
     total = jnp.concatenate(planes, 1)
-    high = total.astype(BF)
-    low = (total - high.astype(F32)).astype(BF)
-    mixed = dot_nt(fold, high) + dot_nt(fold, low)
+    mixed = dot_nt(fold, total.astype(BF))
     return jnp.concatenate([mixed[:64], mixed[64:]], 1)
 
 
@@ -200,12 +198,12 @@
 ):
     row = lax.axis_index("row")
     aisle = lax.axis_index("aisle")
-    held = (row - 2 * aisle + NR) % NR
-    quad = held // 2
-    half = row % 2
-    place = aisle // 2
-    side = aisle % 2
-    group = aisle % 8
+    held = (row - 2 * aisle) & (NR - 1)
+    quad = held >> 1
+    half = row & 1
+    place = aisle >> 1
+    side = aisle & 1
+    group = aisle & 7
 
     loads = [pltpu.make_async_copy(flow_hbm, flow, load_sem.at[0])]
     for i, (first, last) in enumerate(GROUPS):
@@ -220,14 +218,14 @@
     barrier = pltpu.get_barrier_semaphore()
 
     def away(i):
-        return (12 + (i + 1) // 2 * (1 - 2 * (i % 2))) % 8
+        return (12 + ((i + 1) >> 1) * (1 - 2 * (i & 1))) & 7
 
     def row_at(i):
-        low = (row // 16 + 1 - i % 4 // 2) % 2
-        return low * 16 + (row // 2 + away(i // 4)) % 8 * 2 + (row + 1 - i % 2) % 2
+        low = ((row >> 4) + 1 + (i >> 1)) & 1
+        return low * 16 + (((row >> 1) + away(i >> 2)) & 7) * 2 + ((row + 1 + i) & 1)
 
     def aisle_at(step, other):
-        return (place + step + 8) % 8 * 2 + (side + other) % 2
+        return ((place + step) & 7) * 2 + ((side + other) & 1)
 
     for step in (-3, -2, -1, 1, 0):
         for other in (1, 0):
@@ -271,7 +269,7 @@
         for other in (1, 0):
             to = aisle_at(step, other)
             if step or other:
-                remote(0, send_a.at[to % 8], recv_a.at[group], (row, to))
+                remote(0, send_a.at[to & 7], recv_a.at[group], (row, to))
     local(0, send_a.at[group], recv_a.at[group])
 
     ending.append(lambda: sent(0, send_a.at[pl.ds(0, 7)]))
@@ -303,7 +301,7 @@
     @pl.loop(0, NR - 1)
     def _(i):
         to = row_at(i)
-        pair = (to - 2 * aisle + NR) % NR
+        pair = (to - 2 * aisle) & (NR - 1)
         remote(1, send_b.at[:, pair], recv_b.at[:, row], (to, aisle))
 
     local(1, send_b.at[:, held], recv_b.at[:, row])
@@ -368,18 +366,18 @@
 
     @pl.loop(0, 32)
     def _(i):
-        h = i % 2
-        to = (place + away(i // 4)) % 8 * 2 + (side + 1 - i % 4 // 2) % 2
-        target_row = (aisle + to) % 16 * 2 + h
+        h = i & 1
+        to = ((place + away(i >> 2)) & 7) * 2 + ((side + 1 + (i >> 1)) & 1)
+        target_row = ((aisle + to) & 15) * 2 + h
         same = jnp.logical_and(target_row == row, to == aisle)
 
         @pl.when(same)
         def _():
-            local(3, send_d.at[h, :, to % 8], recv_d.at[:, row])
+            local(3, send_d.at[h, :, to & 7], recv_d.at[:, row])
 
         @pl.when(jnp.logical_not(same))
         def _():
-            remote(3, send_d.at[h, :, to % 8], recv_d.at[:, row], (target_row, to))
+            remote(3, send_d.at[h, :, to & 7], recv_d.at[:, row], (target_row, to))
 
     @ending.append
     def _():
@@ -421,7 +419,7 @@
         for other in (1, 0):
             to = aisle_at(step, other)
             if step or other:
-                remote(5, send_f.at[to % 8], recv_f.at[group], (row, to))
+                remote(5, send_f.at[to & 7], recv_f.at[group], (row, to))
     local(5, send_f.at[group], recv_f.at[group])
 
     ending.append(lambda: sent(5, send_f.at[pl.ds(0, 7)]))

time: 54.8 us -> 53.8 us (0.982)
  Pallas kernels: 53.9 us -> 52.9 us
    pallas_call x1, Pallas kernels: 53.9 us -> 52.9 us  [on_device(): pl.pallas_call(kernel, out_shape=pltpu.VMEM(flow_state.shape, BF), in_spe...]
where the time goes in v5:
time: 53.8 us; the launch traced here: 53.7 us
  Pallas kernels  52.9 us (98%)
  local copies, waits for them, and re-layouts  0.8 us (1%)
    pallas_call x1, Pallas kernels, on_device(): pl.pallas_call(kernel, out_shape=pltpu.VMEM(flow_state.shape, BF), in_spe...  52.9 us

profile of v5, /device:TPU:1, one launch (start us, length us, event | category | flops | bytes accessed | tf_op | source)
XLA Modules:
  0.0 53.7 jit_solution(6539836425086315506)
XLA Ops:
  0.0 52.9 %fourier_layer.1 = bf16[2,16,32,256]{3,2,1,0:T(8,128)(2,1)S(1)} custom-call(bf16[2,16,32,256]{3,2,1,0:T(8,128)(2,1)} %refs_0_.1, bf16[2,2,4,32,1024]{4,3,2,1,0:T(8,128)(2,1)} %refs_1_.1, bf16[32,32]{1,0:T(8,128)(2,1)} %refs_2_.1, f32[1,32]{1,0:T(1,128)} %bitcast.1, bf16[3712,256]{1,0:T(8,128)(2,1)} %constant.2.clone.refs_4_), custom_call_target="tpu_custom_call" | custom-call | tf_op jit(solution)/shard_map/fourier_layer/pallas_call | solution.py:454
  52.9 0.8 %copy.7 = bf16[2,16,32,256]{3,2,1,0:T(8,128)(2,1)} copy(bf16[2,16,32,256]{3,2,1,0:T(8,128)(2,1)S(1)} %fourier_layer.1) | data formatting | bytes 1048576

commit v6 on v5

--- a/solution.py
+++ b/solution.py
@@ -152,8 +152,8 @@
                 for h in range(4):
                     mr = wide[rows, h * 128 : h * 128 + 128]
                     mi = wide[rows, 512 + h * 128 : 512 + h * 128 + 128]
-                    wr = weight(0, p, q, c * 512 + h * 128).astype(F32)
-                    wi = weight(1, p, q, c * 512 + h * 128).astype(F32)
+                    wr = weight(0, p, q, c * 512 + h * 128)
+                    wi = weight(1, p, q, c * 512 + h * 128)
                     re = mr * wr - mi * wi
                     im = mr * wi + mi * wr
                     real[q] = re if real[q] is None else real[q] + re
@@ -192,7 +192,7 @@
 def stages(
     flow_hbm, weight_hbm, bypass_hbm, bias_hbm, table_hbm,
     out,
-    flow, weight, bypass, bias, table,
+    flow, weight, wide_weight, bypass, bias, table,
     send_a, recv_a, send_b, recv_b, send_c, recv_c, send_d, recv_d, send_e, recv_e, send_f, recv_f,
     plain, send_sem, recv_sem, own_sem, load_sem, ending,
 ):
@@ -212,9 +212,6 @@
     loads.append(pltpu.make_async_copy(bypass_hbm, bypass, load_sem.at[5]))
     loads.append(pltpu.make_async_copy(bias_hbm, bias, load_sem.at[6]))
     loads.append(pltpu.make_async_copy(weight_hbm, weight, load_sem.at[7]))
-    for load in loads:
-        load.start()
-
     barrier = pltpu.get_barrier_semaphore()
 
     def away(i):
@@ -236,6 +233,9 @@
     @pl.loop(0, NR - 1)
     def _(i):
         pl.semaphore_signal(barrier, inc=1, device_id=(row_at(i), aisle), device_id_type=MESH)
+
+    for load in loads:
+        load.start()
 
     def tile(first, rows=256):
         return table[first : first + rows]
@@ -345,6 +345,7 @@
         def _():
             pltpu.make_async_copy(send_c.at[:, 0], send_c.at[:, 0], own_sem).wait()
 
+    wide_weight[...] = weight[...].astype(F32)
     arrived(2, recv_c)
     yield
 
@@ -360,7 +361,7 @@
             jnp.concatenate(modes, 0).astype(BF),
             spread,
             fold,
-            lambda r, p, q, lane: weight[r, p, 2 * h + q, :, lane : lane + 128],
+            lambda r, p, q, lane: wide_weight[r, p, 2 * h + q, :, lane : lane + 128],
         )
         send_d.reshape(128, 128)[h * 64 : h * 64 + 64] = mixed.astype(BF)
 
@@ -459,6 +460,7 @@
         scratch_shapes=[
             pltpu.VMEM(flow_state.shape, BF),
             pltpu.VMEM(mode_weight.shape, BF),
+            pltpu.VMEM(mode_weight.shape, F32),
             pltpu.VMEM(bypass_weight.shape, BF),
             pltpu.VMEM((1, C), F32),
             pltpu.VMEM((ROWS, 256), BF),

time: 53.8 us -> 53.6 us (level)
  no operation moved by 1% of the time
where the time goes in v6:
time: 53.6 us; the launch traced here: 53.5 us
  Pallas kernels  52.7 us (98%)
  local copies, waits for them, and re-layouts  0.8 us (1%)
    pallas_call x1, Pallas kernels, on_device(): pl.pallas_call(kernel, out_shape=pltpu.VMEM(flow_state.shape, BF), in_spe...  52.7 us

profile of v6, /device:TPU:1, one launch (start us, length us, event | category | flops | bytes accessed | tf_op | source)
XLA Modules:
  0.0 53.5 jit_solution(11374244290097861332)
XLA Ops:
  0.0 52.7 %fourier_layer.1 = bf16[2,16,32,256]{3,2,1,0:T(8,128)(2,1)S(1)} custom-call(bf16[2,16,32,256]{3,2,1,0:T(8,128)(2,1)} %refs_0_.1, bf16[2,2,4,32,1024]{4,3,2,1,0:T(8,128)(2,1)} %refs_1_.1, bf16[32,32]{1,0:T(8,128)(2,1)} %refs_2_.1, f32[1,32]{1,0:T(1,128)} %bitcast.1, bf16[3712,256]{1,0:T(8,128)(2,1)} %constant.2.clone.refs_4_), custom_call_target="tpu_custom_call" | custom-call | tf_op jit(solution)/shard_map/fourier_layer/pallas_call | solution.py:455
  52.7 0.8 %copy.7 = bf16[2,16,32,256]{3,2,1,0:T(8,128)(2,1)} copy(bf16[2,16,32,256]{3,2,1,0:T(8,128)(2,1)S(1)} %fourier_layer.1) | data formatting | bytes 1048576
